TPU v7x, 32 devices: a whole 2x2x4 slice. The times are simulated.
32 devices in a mesh: pole: 4 (over y, x), row: 2 (over core), col: 4 (over z).
Axes of the slice: x: 2, y: 2, z: 4, core: 2. Of those that a mesh axis runs over, the one named last changes fastest.
Arguments:
- hamiltonian_panel: bfloat16 [6144, 512], P(('row', 'col'), 'pole'), may hold values from -0.005859375 to 0.005859375
- margin_panel: bfloat16 [6144, 512], P(('row', 'col'), 'pole'), may hold values from -0.0029296875 to 0.0029296875
- shifts: float32 [4, 2], P('pole'), may hold values from -2 to 2
- weights: float32 [4, 2], P('pole'), may hold values from 0.5 to 2
- pivot_inverse: float32 [4, 2, 512, 512], P('pole'), may hold values from -6 to 6
- selected_inverse: bfloat16 [4, 2, 6144, 6144], P('pole', None, 'row', 'col'), may hold values from -6 to 6
Outputs:
- inverse_column: float32 [4, 6144, 2, 512], P('pole', ('row', 'col'))
- inverse_pivot: float32 [4, 2, 512, 512], P('pole')
- density_column: float32 [6144, 512], P(('row', 'col'), 'pole')
- density_pivot: float32 [512, 512], P('pole')
All inputs are finite; a program needn't handle non-finite values.
Results may differ from a plain program's by a relative error of at most 0.0037.
Values may be sent and summed in bfloat16 or wider, within the bound.
A program may use at most 128 MiB of HBM per device.

v0:
```python
import jax
import jax.numpy as jnp
from jax import lax
from jax.sharding import PartitionSpec as P

PANEL = 512


def precise(left, right):
    return jnp.dot(left, right, precision=lax.Precision.HIGHEST, preferred_element_type=jnp.float32)


def factor_panel(hamiltonian, margin, shift, inverse):
    hamiltonian_f = hamiltonian.astype(jnp.float32)
    margin_f = margin.astype(jnp.float32)
    real_part = hamiltonian_f - shift[0] * margin_f
    imag_part = -shift[1] * margin_f
    lower_real = precise(real_part, inverse[0]) - precise(imag_part, inverse[1])
    lower_imag = precise(real_part, inverse[1]) + precise(imag_part, inverse[0])
    return jnp.stack([lower_real, lower_imag], axis=1).astype(jnp.bfloat16)


def apply_block(block_real, block_imag, lower):
    width = lower.shape[2]
    flat = lower.reshape(lower.shape[0], 2 * width)
    first = jnp.dot(block_real, flat, preferred_element_type=jnp.float32)
    second = jnp.dot(block_imag, flat, preferred_element_type=jnp.float32)
    return -jnp.stack(
        [first[:, :width] - second[:, width:], first[:, width:] + second[:, :width]], axis=1
    )


def pivot_term(lower, column):
    width = lower.shape[2]
    left = lower.astype(jnp.float32).reshape(lower.shape[0], 2 * width)
    right = column.reshape(column.shape[0], 2 * width)
    square = lax.dot_general(
        left,
        right,
        (((0,), (0,)), ((), ())),
        precision=lax.Precision.HIGHEST,
        preferred_element_type=jnp.float32,
    )
    return jnp.stack(
        [
            square[:width, :width] - square[width:, width:],
            square[:width, width:] + square[width:, :width],
        ]
    )


def body(hamiltonian_panel, margin_panel, shifts, weights, pivot_inverse, selected_inverse):
    shift = shifts[0]
    weight = weights[0]
    inverse = pivot_inverse[0]
    block = selected_inverse[0]
    span = block.shape[2]
    column_index = lax.axis_index("col")
    both = (
        lax.all_gather(hamiltonian_panel, "pole", axis=1, tiled=True),
        lax.all_gather(margin_panel, "pole", axis=1, tiled=True),
    )
    owned = factor_panel(both[0], both[1], shift, inverse)
    gathered = lax.all_gather(owned, ("row", "col"), axis=0, tiled=True)
    needed = lax.dynamic_slice_in_dim(gathered, column_index * span, span, 0)
    block_real = block[0]
    block_imag = block[1]
    column = lax.psum_scatter(
        apply_block(block_real, block_imag, needed), "col", scatter_dimension=0, tiled=True
    )
    pivot = inverse - lax.psum(pivot_term(owned, column), ("row", "col"))
    column_density = weight[0] * column[:, 0] - weight[1] * column[:, 1]
    pivot_density = weight[0] * pivot[0] - weight[1] * pivot[1]
    totals = lax.psum((column_density, pivot_density), "pole")
    portion = PANEL // lax.axis_size("pole")
    slot = lax.axis_index("pole")
    column_share = lax.dynamic_slice_in_dim(totals[0], slot * portion, portion, 1)
    pivot_share = lax.dynamic_slice_in_dim(totals[1], slot * portion, portion, 0)
    return (column[None], pivot[None], column_share, pivot_share)


def solution(mesh):
    return jax.shard_map(
        body,
        mesh=mesh,
        in_specs=(
            P(("row", "col"), "pole"),
            P(("row", "col"), "pole"),
            P("pole", None),
            P("pole", None),
            P("pole", None, None, None),
            P("pole", None, "row", "col"),
        ),
        out_specs=(
            P("pole", ("row", "col"), None, None),
            P("pole", None, None, None),
            P(("row", "col"), "pole"),
            P("pole", None),
        ),
        check_vma=False,
    )
```

profile of v0, /device:TPU:0, one launch (start us, length us, event | category | flops | bytes accessed | tf_op | source)
XLA Modules:
  0.0 594.3 jit_solution(16487910491604722457)
XLA Ops:
  7.2 13.8 %all_gather.10 = bf16[768,512]{1,0:T(8,128)(2,1)S(1)} all-gather(bf16[768,128]{1,0:T(8,128)(2,1)} %param.7), channel_id=1, replica_groups=mesh['pole'=4,'row'=2,'col'=4] {'pole'}, dimensions={1}, use_global_device_ids=true | all-gather | bytes 983040 | tf_op jit(solution)/shard_map/all_gather | solution.py:61
  21.0 1.3 fusion.42
  22.3 11.1 %all_gather.9 = bf16[768,512]{1,0:T(8,128)(2,1)S(1)} all-gather(bf16[768,128]{1,0:T(8,128)(2,1)} %param.6), channel_id=1, replica_groups=mesh['pole'=4,'row'=2,'col'=4] {'pole'}, dimensions={1}, use_global_device_ids=true | all-gather | bytes 983040 | tf_op jit(solution)/shard_map/all_gather | solution.py:60
  33.4 5.0 fusion.21
  38.4 3.7 fusion.19
  42.8 3.1 fusion.23
  45.8 3.1 fusion.24
  48.9 1.5 pad_maximum_fusion.1
  50.4 117.1 %all-gather.2.cloned.1.call-done = bf16[6144,2,512]{0,2,1:T(8,128)(2,1)} async-done(((bf16[768,2,512]{0,2,1:T(8,128)(2,1)}), bf16[6144,2,512]{0,2,1:T(8,128)(2,1)}) %all-gather.2.cloned.1.call-update) | async-done | bytes 12582928 | tf_op jit(solution)/shard_map/all_gather | solution.py:64
  167.5 2.1 constant_dynamic-slice_fusion.2
  169.6 12.5 %fusion.6 = f32[3072,1024]{0,1:T(8,128)S(1)} fusion(bf16[1536,1024]{0,1:T(8,128)(2,1)S(1)} %bitcast.59, bf16[1,2,3072,1536]{3,2,1,0:T(8,128)(2,1)} %param.11), kind=kOutput, calls=%fused_computation.7 | convolution fusion | flops 9663676416 | bytes 25165824 | tf_op jit(solution)/shard_map/dot_general | solution.py:26
  182.1 15.2 %fusion.9 = f32[3072,1024]{0,1:T(8,128)} fusion(bf16[1536,1024]{0,1:T(8,128)(2,1)S(1)} %bitcast.60, bf16[1,2,3072,1536]{3,2,1,0:T(8,128)(2,1)} %param.11), kind=kOutput, calls=%fused_computation.8 | convolution fusion | flops 9663676416 | bytes 25165824 | tf_op jit(solution)/shard_map/dot_general | solution.py:27
  197.3 7.4 %fusion.13 = (f32[3072,1,512]{0,2,1:T(8,128)S(1)}, f32[3072,1,512]{0,2,1:T(8,128)}) fusion(f32[3072,1024]{0,1:T(8,128)} %fusion.9, f32[3072,1024]{0,1:T(8,128)S(1)} %fusion.6), kind=kLoop, calls=%fused_computation.12 | loop fusion | flops 3145728 | bytes 37748736 | tf_op jit(solution)/shard_map/stack | solution.py:28
  204.8 9.2 %maximum_negate_fusion = f32[3072,2,512]{0,2,1:T(8,128)} fusion(f32[3072,1,512]{0,2,1:T(8,128)} %get-tuple-element.11, f32[3072,1,512]{0,2,1:T(8,128)S(1)} %get-tuple-element.10), kind=kLoop, calls=%fused_computation | loop fusion | flops 6291456 | bytes 25165824 | tf_op jit(solution)/shard_map/neg | solution.py:28
  214.0 0.3 all-reduce.4.cloned.1.call-start
  214.2 209.9 %reduce-scatter.2.cloned.1.call-done = f32[768,2,512]{0,2,1:T(8,128)} async-done(((f32[3072,2,512]{0,2,1:T(8,128)}), f32[768,2,512]{0,2,1:T(8,128)}) %reduce-scatter.2.cloned.1.call-update) | async-done | bytes 3145744 | tf_op jit(solution)/shard_map/reduce_scatter | solution.py:68
  424.2 7.1 %fusion.43 = f32[1024,1024]{1,0:T(8,128)S(1)} fusion(bf16[768,1024]{0,1:T(8,128)(2,1)S(1)} %bitcast.58, f32[768,1024]{0,1:T(8,128)} %bitcast.55), kind=kOutput, calls=%fused_computation.56 | convolution fusion | flops 9663676416 | bytes 8912896 | tf_op jit(solution)/shard_map/dot_general | solution.py:37
  431.3 0.5 fusion.28
  431.8 1.5 pad_maximum_fusion
  433.4 0.0 all-reduce.6.cloned.1.call-start
  433.4 0.6 copy-done.5
  434.0 0.6 fusion.41
  434.6 4.7 fusion.18
  439.3 60.3 %all-reduce.4.cloned.1.call-done = f32[2,512,512]{2,1,0:T(8,128)} async-done(((f32[2,512,512]{2,1,0:T(8,128)}), f32[2,512,512]{2,1,0:T(8,128)}) %all-reduce.4.cloned.1.call-update) | async-done | bytes 2097168 | tf_op jit(solution)/shard_map/psum | solution.py:71
  499.5 2.1 bitcast_subtract_fusion
  501.6 1.3 copy-done.3
  502.9 2.8 fusion.26
  505.8 3.4 copy.10
  509.1 75.0 %all-reduce.6.cloned.1.call-done = (f32[768,512]{0,1:T(8,128)}, f32[512,512]{1,0:T(8,128)}) async-done(((f32[768,512]{0,1:T(8,128)}, f32[512,512]{1,0:T(8,128)}), (f32[768,512]{0,1:T(8,128)}, f32[512,512]{1,0:T(8,128)})) %all-reduce.6.cloned.1.call-update) | async-done | bytes 2621456 | tf_op jit(solution)/shard_map/psum | solution.py:74
  584.2 1.0 constant_dynamic-slice_fusion.1
  585.2 0.9 copy.11
  586.1 1.7 constant_dynamic-slice_fusion
  (16 shorter events, 0.2 us)
Async XLA Ops:
  7.2 160.4 %all-gather.2.cloned.1.call-start = ((), (), s32[]{:S(2)}) async-start(), calls=%async_computation.1 | async-start | bytes 14155776 | tf_op jit(solution)/shard_map/all_gather | solution.py:64
  33.4 5.0 copy-start
  50.4 373.8 %reduce-scatter.2.cloned.1.call-start = ((), (), s32[]{:S(2)}) async-start(), calls=%async_computation.2 | async-start | bytes 15728640 | tf_op jit(solution)/shard_map/reduce_scatter | solution.py:68
  213.9 210.2 %copy-start.4 = (bf16[768,2,512]{0,2,1:T(8,128)(2,1)S(1)}, bf16[768,2,512]{0,2,1:T(8,128)(2,1)}, u32[]{:S(2)}) copy-start(bf16[768,2,512]{0,2,1:T(8,128)(2,1)} %pad_maximum_fusion.1) | copy-start | bytes 4718596
  214.0 285.5 %all-reduce.4.cloned.1.call-start = ((), (), s32[]{:S(2)}) async-start(), calls=%async_computation.3 | async-start | bytes 4194304 | tf_op jit(solution)/shard_map/psum | solution.py:71
  433.3 0.7 copy-start.5
  433.4 150.8 %all-reduce.6.cloned.1.call-start = ((), (), s32[]{:S(2)}) async-start(), calls=%async_computation.4 | async-start | bytes 5242880 | tf_op jit(solution)/shard_map/psum | solution.py:74
  434.6 64.9 %copy-start.1 = (f32[1,2,512,512]{3,2,1,0:T(8,128)S(1)}, f32[1,2,512,512]{3,2,1,0:T(8,128)}, u32[]{:S(2)}) copy-start(f32[1,2,512,512]{3,2,1,0:T(8,128)} %param.10) | copy-start | bytes 6291460
  501.6 1.3 copy-start.3
  502.9 2.9 copy-start.2
Sparse Core Ops, SparseCore 0:
  50.5 116.9 all-gather.1
  214.1 210.0 reduce-scatter.1
  433.5 65.9 all-reduce.3
  505.9 78.2 all-reduce.5
where the time goes:
time: 595 us; the launch traced here: 594 us
  waiting for transfers between devices  462 us (78%)
  matrix products  49.6 us (8%)
  other arithmetic  29.7 us (5%)
  blocking collectives  24.9 us (4%)
  between operations  14.5 us (2%)
  local copies, waits for them, and re-layouts  12.9 us (2%)
    reduce_scatter x1, waiting for transfers between devices, body(): lax.psum_scatter(apply_block(block_real, block_imag, needed), 'col', scat...  210 us
    all_gather x1, waiting for transfers between devices, body(): gathered = lax.all_gather(owned, ('row', 'col'), axis=0, tiled=True)  117 us
    psum x1, waiting for transfers between devices, body(): totals = lax.psum((column_density, pivot_density), 'pole')  75 us
    psum x1, waiting for transfers between devices, body(): pivot = inverse - lax.psum(pivot_term(owned, column), ('row', 'col'))  60.3 us
    dot_general x1, matrix products, apply_block(): second = jnp.dot(block_imag, flat, preferred_element_type=jnp.float32)  15.2 us
    dot_general x4, matrix products, precise(): jnp.dot(left, right, precision=lax.Precision.HIGHEST, preferred_element_t...  14.8 us
    all_gather x1, blocking collectives, body(): lax.all_gather(margin_panel, 'pole', axis=1, tiled=True)  13.8 us
    dot_general x1, matrix products, apply_block(): first = jnp.dot(block_real, flat, preferred_element_type=jnp.float32)  12.5 us
  transfers between devices with their start and end apart: 4, of which 4 were waited for; matrix products, arithmetic and copies ran while one was open for 1% of the time, Pallas kernels for 0%

commit v1 on v0

--- a/solution.py
+++ b/solution.py
@@ -68,7 +68,7 @@
     column = lax.psum_scatter(
         apply_block(block_real, block_imag, needed), "col", scatter_dimension=0, tiled=True
     )
-    pivot = inverse - lax.psum(pivot_term(owned, column), ("row", "col"))
+    pivot = inverse - jnp.sum(lax.all_gather(pivot_term(owned, column), ("row", "col")), axis=0)
     column_density = weight[0] * column[:, 0] - weight[1] * column[:, 1]
     pivot_density = weight[0] * pivot[0] - weight[1] * pivot[1]
     totals = lax.psum((column_density, pivot_density), "pole")

time: 595 us -> 691 us (1.16)
  waiting for transfers between devices: 462 us -> 541 us
  other arithmetic: 29.7 us -> 45.4 us
    all_gather x0 -> x1, waiting for transfers between devices: none -> 147 us  [body(): lax.all_gather(pivot_term(owned, column), ('row', 'col'))]
    psum x1 -> x0, waiting for transfers between devices: 60.3 us -> none  [body(): pivot = inverse - lax.psum(pivot_term(owned, column), ('row', 'col'))]
    reduce_sum x0 -> x1, other arithmetic: none -> 9.4 us  [body(): jnp.sum(lax.all_gather(pivot_term(owned, column), ('row', 'col')), axis=0)]
    psum x1, waiting for transfers between devices: 75 us -> 67.7 us  [body(): totals = lax.psum((column_density, pivot_density), 'pole')]
  transfers between devices with their start and end apart: 4 -> 4, of which waited for: 4 -> 4; matrix products, arithmetic and copies ran while one was open for 1% -> 2% of each run, Pallas kernels for 0% -> 0%
where the time goes in v1:
time: 691 us; the launch traced here: 690 us
  waiting for transfers between devices  541 us (78%)
  matrix products  49.6 us (7%)
  other arithmetic  45.4 us (7%)
  blocking collectives  24.9 us (4%)
  between operations  14.5 us (2%)
  local copies, waits for them, and re-layouts  14.1 us (2%)
    reduce_scatter x1, waiting for transfers between devices, body(): lax.psum_scatter(apply_block(block_real, block_imag, needed), 'col', scat...  210 us
    all_gather x1, waiting for transfers between devices, body(): lax.all_gather(pivot_term(owned, column), ('row', 'col'))  147 us
    all_gather x1, waiting for transfers between devices, body(): gathered = lax.all_gather(owned, ('row', 'col'), axis=0, tiled=True)  117 us
    psum x1, waiting for transfers between devices, body(): totals = lax.psum((column_density, pivot_density), 'pole')  67.7 us
    dot_general x1, matrix products, apply_block(): second = jnp.dot(block_imag, flat, preferred_element_type=jnp.float32)  15.1 us
    dot_general x4, matrix products, precise(): jnp.dot(left, right, precision=lax.Precision.HIGHEST, preferred_element_t...  14.4 us
  transfers between devices with their start and end apart: 4, of which 4 were waited for; matrix products, arithmetic and copies ran while one was open for 2% of the time, Pallas kernels for 0%

profile of v1, /device:TPU:0, one launch (start us, length us, event | category | flops | bytes accessed | tf_op | source)
XLA Modules:
  0.0 690.3 jit_solution(1827289699413991197)
XLA Ops:
  7.2 13.8 %all_gather.16 = bf16[768,512]{1,0:T(8,128)(2,1)S(1)} all-gather(bf16[768,128]{1,0:T(8,128)(2,1)} %param.7), channel_id=1, replica_groups=mesh['pole'=4,'row'=2,'col'=4] {'pole'}, dimensions={1}, use_global_device_ids=true | all-gather | bytes 983040 | tf_op jit(solution)/shard_map/all_gather | solution.py:61
  21.0 1.3 fusion.42
  22.3 11.1 %all_gather.15 = bf16[768,512]{1,0:T(8,128)(2,1)S(1)} all-gather(bf16[768,128]{1,0:T(8,128)(2,1)} %param.6), channel_id=1, replica_groups=mesh['pole'=4,'row'=2,'col'=4] {'pole'}, dimensions={1}, use_global_device_ids=true | all-gather | bytes 983040 | tf_op jit(solution)/shard_map/all_gather | solution.py:60
  33.4 5.0 fusion.21
  38.4 3.6 fusion.19
  42.6 2.9 fusion.23
  45.6 2.9 fusion.24
  48.5 1.5 pad_maximum_fusion.1
  50.0 117.1 %all-gather.4.cloned.1.call-done = bf16[6144,2,512]{0,2,1:T(8,128)(2,1)} async-done(((bf16[768,2,512]{0,2,1:T(8,128)(2,1)}), bf16[6144,2,512]{0,2,1:T(8,128)(2,1)}) %all-gather.4.cloned.1.call-update) | async-done | bytes 12582928 | tf_op jit(solution)/shard_map/all_gather | solution.py:64
  167.1 2.1 constant_dynamic-slice_fusion.2
  169.2 12.5 %fusion.6 = f32[3072,1024]{0,1:T(8,128)S(1)} fusion(bf16[1536,1024]{0,1:T(8,128)(2,1)S(1)} %bitcast.61, bf16[1,2,3072,1536]{3,2,1,0:T(8,128)(2,1)} %param.11), kind=kOutput, calls=%fused_computation.7 | convolution fusion | flops 9663676416 | bytes 25165824 | tf_op jit(solution)/shard_map/dot_general | solution.py:26
  181.7 15.1 %fusion.9 = f32[3072,1024]{0,1:T(8,128)} fusion(bf16[1536,1024]{0,1:T(8,128)(2,1)S(1)} %bitcast.62, bf16[1,2,3072,1536]{3,2,1,0:T(8,128)(2,1)} %param.11), kind=kOutput, calls=%fused_computation.8 | convolution fusion | flops 9663676416 | bytes 25165824 | tf_op jit(solution)/shard_map/dot_general | solution.py:27
  196.8 8.5 %fusion.13 = (f32[3072,1,512]{0,2,1:T(8,128)}, f32[3072,1,512]{0,2,1:T(8,128)}) fusion(f32[3072,1024]{0,1:T(8,128)} %fusion.9, f32[3072,1024]{0,1:T(8,128)S(1)} %fusion.6), kind=kLoop, calls=%fused_computation.12 | loop fusion | flops 3145728 | bytes 37748736 | tf_op jit(solution)/shard_map/stack | solution.py:28
  205.3 11.6 %maximum_negate_fusion = f32[3072,2,512]{0,2,1:T(8,128)} fusion(f32[3072,1,512]{0,2,1:T(8,128)} %get-tuple-element.15, f32[3072,1,512]{0,2,1:T(8,128)} %get-tuple-element.14), kind=kLoop, calls=%fused_computation | loop fusion | flops 6291456 | bytes 25165824 | tf_op jit(solution)/shard_map/neg | solution.py:28
  216.9 0.3 all-gather.6.cloned.1.call-start
  217.2 209.9 %reduce-scatter.2.cloned.1.call-done = f32[768,2,512]{0,2,1:T(8,128)} async-done(((f32[3072,2,512]{0,2,1:T(8,128)}), f32[768,2,512]{0,2,1:T(8,128)}) %reduce-scatter.2.cloned.1.call-update) | async-done | bytes 3145744 | tf_op jit(solution)/shard_map/reduce_scatter | solution.py:68
  427.1 7.6 %fusion.43 = f32[1024,1024]{1,0:T(8,128)S(1)} fusion(bf16[768,1024]{0,1:T(8,128)(2,1)} %bitcast.60, f32[768,1024]{0,1:T(8,128)} %bitcast.58), kind=kOutput, calls=%fused_computation.57 | convolution fusion | flops 9663676416 | bytes 8912896 | tf_op jit(solution)/shard_map/dot_general | solution.py:37
  434.7 0.5 fusion.28
  435.2 1.5 pad_maximum_fusion
  436.8 0.6 copy-done.1
  437.4 0.6 fusion.41
  438.0 4.5 fusion.18
  442.5 146.6 %all-gather.6.cloned.1.call-done = f32[16,512,512]{2,1,0:T(8,128)} async-done(((f32[2,512,512]{2,1,0:T(8,128)}), f32[16,512,512]{2,1,0:T(8,128)}) %all-gather.6.cloned.1.call-update) | async-done | bytes 16777232 | tf_op jit(solution)/shard_map/all_gather | solution.py:71
  589.1 9.4 %reduce_sum.11 = f32[2,512,512]{2,1,0:T(8,128)} reduce(f32[8,2,512,512]{3,2,1,0:T(8,128)} %bitcast.57, f32[]{:T(128)} %constant.5.clone.1), dimensions={0}, to_apply=%region_1.0 | reduce | flops 3670016 | bytes 18874372 | tf_op jit(solution)/shard_map/reduce_sum | solution.py:71
  598.5 2.1 bitcast_subtract_fusion
  600.6 2.5 fusion.26
  603.1 5.9 copy.12
  609.0 3.4 bitcast_subtract_fusion.1
  612.4 67.7 %all-reduce.3.cloned.1.call-done = (f32[768,512]{0,1:T(8,128)}, f32[512,512]{1,0:T(8,128)}) async-done(((f32[768,512]{0,1:T(8,128)}, f32[512,512]{1,0:T(8,128)}), (f32[768,512]{0,1:T(8,128)}, f32[512,512]{1,0:T(8,128)})) %all-reduce.3.cloned.1.call-update) | async-done | bytes 2621456 | tf_op jit(solution)/shard_map/psum | solution.py:74
  680.1 1.0 constant_dynamic-slice_fusion.1
  681.1 0.9 copy.13
  682.1 1.7 constant_dynamic-slice_fusion
  (10 shorter events, 0.2 us)
Async XLA Ops:
  7.2 160.0 %all-gather.4.cloned.1.call-start = ((), (), s32[]{:S(2)}) async-start(), calls=%async_computation.1 | async-start | bytes 14155776 | tf_op jit(solution)/shard_map/all_gather | solution.py:64
  33.4 5.0 copy-start
  50.0 377.2 %reduce-scatter.2.cloned.1.call-start = ((), (), s32[]{:S(2)}) async-start(), calls=%async_computation.2 | async-start | bytes 15728640 | tf_op jit(solution)/shard_map/reduce_scatter | solution.py:68
  216.9 372.2 %all-gather.6.cloned.1.call-start = ((), (), s32[]{:S(2)}) async-start(), calls=%async_computation.3 | async-start | bytes 18874368 | tf_op jit(solution)/shard_map/all_gather | solution.py:71
  436.8 0.7 copy-start.1
  436.8 243.3 %all-reduce.3.cloned.1.call-start = ((), (), s32[]{:S(2)}) async-start(), calls=%async_computation.4 | async-start | bytes 5242880 | tf_op jit(solution)/shard_map/psum | solution.py:74
Sparse Core Ops, SparseCore 0:
  50.1 116.9 all-gather.3
  217.0 210.0 reduce-scatter.1
  436.9 152.1 all-gather.5
  603.2 76.8 all-reduce.2
